TPU v7x, 32 devices: a whole 2x2x4 slice. The times are simulated.
32 devices in a mesh: groups: 2 (over y), ctx: 4 (over z), head: 4 (over x, core).
Axes of the slice: x: 2, y: 2, z: 4, core: 2. Of those that a mesh axis runs over, the one named last changes fastest.
Arguments:
- query_rows: bfloat16 [4096, 4096], P(('groups', 'ctx', 'head')), parts along dimension 0, may hold values from -6 to 6
- key_rows: bfloat16 [4096, 4096], P(('groups', 'ctx', 'head')), parts along dimension 0, may hold values from -6 to 6
- value_rows: bfloat16 [4096, 8192], P(('groups', 'ctx', 'head')), parts along dimension 0, may hold values from -30 to 30
- gate_rows: bfloat16 [4096, 8192], P(('groups', 'ctx', 'head')), parts along dimension 0, may hold values from -6 to 6
- decay_log: bfloat16 [4096, 16], P(('groups', 'ctx', 'head')), parts along dimension 0, may hold values from -1 to 0, as said below
- norm_gain: float32 [8192], P('head'), may hold values from 0.25 to 1.75
Outputs:
- retention_out: bfloat16 [4096, 8192], P(('groups', 'ctx', 'head')), parts along dimension 0
There are 2 independent parts, one for each index of `groups`. A program takes and returns all parts, laid end to end along the dimension named above; an argument that names none is the same for every part. Nothing has to cross between parts.
Inputs may be any that keep to these rules, and one draw needn't show every extreme that they name: `decay_log`: every entry is negative.
All inputs are finite; a program needn't handle non-finite values.
Results may differ from a plain program's by a relative error of at most 0.0085.
Values may be sent and summed in bfloat16 or wider, within the bound.
A program may use at most 128 MiB of HBM per device.

v0:
```python
import jax
import jax.numpy as jnp
from jax import lax
from jax.sharding import PartitionSpec as P

KEY_DIM = 256
VALUE_DIM = 512


def prefix(x, axis, combine, identity):
    devices, index = (lax.axis_size(axis), lax.axis_index(axis))
    everything = jax.tree.map(lambda part: lax.all_gather(part, axis), x)
    start = jax.tree.map(
        lambda part, zero: jnp.broadcast_to(jnp.asarray(zero, part.dtype), part.shape), x, identity
    )

    def turn(k, before):
        reached = k < index
        new = combine(before, jax.tree.map(lambda part: part[k], everything))
        return jax.tree.map(lambda a, b: jnp.where(reached, a, b), new, before)

    return lax.fori_loop(0, devices, turn, start)


def merge_states(earlier, latter):
    return (earlier[0] + latter[0], jnp.exp(latter[0])[:, None, None] * earlier[1] + latter[1])


def split_parts(matrix):
    upper = matrix.astype(jnp.bfloat16)
    rest = matrix - lax.optimization_barrier(upper).astype(jnp.float32)
    middle = rest.astype(jnp.bfloat16)
    lowest = (rest - lax.optimization_barrier(middle).astype(jnp.float32)).astype(jnp.bfloat16)
    return (upper, middle, lowest)


def body(query_rows, key_rows, value_rows, gate_rows, decay_log, norm_gain):
    query_heads, key_heads, value_heads, gate_heads, decay_heads = (
        lax.all_to_all(query_rows, "head", split_axis=1, concat_axis=0, tiled=True),
        lax.all_to_all(key_rows, "head", split_axis=1, concat_axis=0, tiled=True),
        lax.all_to_all(value_rows, "head", split_axis=1, concat_axis=0, tiled=True),
        lax.all_to_all(gate_rows, "head", split_axis=1, concat_axis=0, tiled=True),
        lax.all_to_all(decay_log, "head", split_axis=1, concat_axis=0, tiled=True),
    )
    length = query_heads.shape[0]
    local_heads = decay_heads.shape[1]
    query_heads = query_heads.reshape(length, local_heads, KEY_DIM)
    key_heads = key_heads.reshape(length, local_heads, KEY_DIM)
    value_heads = value_heads.reshape(length, local_heads, VALUE_DIM)
    key_scale = KEY_DIM ** (-0.5)
    within = jnp.cumsum(decay_heads.astype(jnp.float32), axis=0)
    block_total = within[-1]
    decayed = (
        key_heads.astype(jnp.float32) * jnp.exp(block_total[None, :] - within)[:, :, None]
    ).astype(jnp.bfloat16)
    block_state = jnp.einsum(
        "jhk,jhd->hkd", decayed, value_heads, preferred_element_type=jnp.float32
    )
    identity = (jnp.zeros_like(block_total), jnp.zeros_like(block_state))
    carried = prefix((block_total, block_state), "ctx", merge_states, identity)[1]
    log_gaps = within.T[:, :, None] - within.T[:, None, :]
    causal = (jnp.arange(length)[:, None] >= jnp.arange(length)[None, :])[None]
    damping = jnp.where(causal, jnp.exp(jnp.where(causal, log_gaps, 0.0)), 0.0)
    scores = jnp.einsum("ihk,jhk->hij", query_heads, key_heads, preferred_element_type=jnp.float32)
    weights = (scores * key_scale * damping).astype(jnp.bfloat16)
    local_out = jnp.einsum("hij,jhd->ihd", weights, value_heads, preferred_element_type=jnp.float32)
    upper, middle, lowest = split_parts(carried)
    inter = jnp.einsum("ihk,hkd->ihd", query_heads, upper, preferred_element_type=jnp.float32)
    inter = inter + jnp.einsum(
        "ihk,hkd->ihd", query_heads, middle, preferred_element_type=jnp.float32
    )
    inter = inter + jnp.einsum(
        "ihk,hkd->ihd", query_heads, lowest, preferred_element_type=jnp.float32
    )
    retained = local_out + inter * (jnp.exp(within) * key_scale)[:, :, None]
    centered = retained - jnp.mean(retained, axis=-1, keepdims=True)
    spread = jnp.mean(centered * centered, axis=-1, keepdims=True)
    normed = (
        centered * lax.rsqrt(spread + 1e-06) * norm_gain.reshape(local_heads, VALUE_DIM)
    ).astype(jnp.bfloat16)
    normed = normed.reshape(length, local_heads * VALUE_DIM)
    mixed = (normed.astype(jnp.float32) * jax.nn.silu(gate_heads.astype(jnp.float32))).astype(
        jnp.bfloat16
    )
    return lax.all_to_all(mixed, "head", split_axis=0, concat_axis=1, tiled=True)


def solution(mesh):
    placed = (
        P(("groups", "ctx", "head"), None),
        P(("groups", "ctx", "head"), None),
        P(("groups", "ctx", "head"), None),
        P(("groups", "ctx", "head"), None),
        P(("groups", "ctx", "head"), None),
        P("head"),
    )
    return jax.shard_map(
        body,
        mesh=mesh,
        in_specs=placed,
        out_specs=P(("groups", "ctx", "head"), None),
        check_vma=False,
    )
```

profile of v0, /device:TPU:0, one launch (start us, length us, event | category | flops | bytes accessed | tf_op | source)
XLA Modules:
  0.0 293.8 jit_solution(11106510641096637045)
XLA Ops:
  6.5 4.2 %all-to-all-start.2 = ((bf16[128,4,4]{0,2,1:T(4,128)(2,1)}), bf16[128,4,4]{0,2,1:T(4,128)(2,1)S(1)}, u32[]{:S(2)}, u32[]{:S(2)}) async-start(bf16[128,4,4]{0,2,1:T(4,128)(2,1)} %bitcast.92), calls=%async_computation.2 | async-start | bytes 8192 | tf_op jit(solution)/shard_map/all_to_all | solution.py:43
  10.7 1.6 copy.91
  12.4 1.3 copy.92
  13.7 0.9 all-to-all-done.2
  14.5 3.5 %all-to-all-start.1 = ((bf16[128,4,1024]{2,0,1:T(8,128)(2,1)}), bf16[128,4,1024]{2,0,1:T(8,128)(2,1)S(1)}, u32[]{:S(2)}, u32[]{:S(2)}) async-start(bf16[128,4,1024]{2,0,1:T(8,128)(2,1)} %copy.92), calls=%async_computation.1 | async-start | bytes 2097152 | tf_op jit(solution)/shard_map/all_to_all | solution.py:40
  18.1 4.1 %copy.95 = bf16[128,8192]{0,1:T(8,128)(2,1)} copy(bf16[128,8192]{1,0:T(8,128)(2,1)} %param.10) | data formatting | bytes 4194304 | tf_op args[2]
  22.1 10.4 %all-to-all-done.1 = bf16[128,4,1024]{2,0,1:T(8,128)(2,1)S(1)} async-done(((bf16[128,4,1024]{2,0,1:T(8,128)(2,1)}), bf16[128,4,1024]{2,0,1:T(8,128)(2,1)S(1)}, u32[]{:S(2)}, u32[]{:S(2)}) %all-to-all-start.1) | async-done | bytes 1048608 | tf_op jit(solution)/shard_map/all_to_all | solution.py:40
  32.5 3.6 %all-to-all-start.3 = ((bf16[128,4,2048]{0,2,1:T(8,128)(2,1)}), bf16[128,4,2048]{0,2,1:T(8,128)(2,1)S(1)}, u32[]{:S(2)}, u32[]{:S(2)}) async-start(bf16[128,4,2048]{0,2,1:T(8,128)(2,1)} %bitcast.7), calls=%async_computation.3 | async-start | bytes 4194304 | tf_op jit(solution)/shard_map/all_to_all | solution.py:41
  36.1 0.0 all-gather.4.cloned.1.call-start
  36.2 1.2 reduce-window.6
  37.4 0.2 slice_reduce_fusion
  37.6 0.2 reduce-window.9
  37.7 0.1 add_bitcast_fusion
  37.8 0.2 slice_reduce_fusion.1
  38.0 0.1 exponential_multiply_fusion
  38.1 0.2 copy.97
  38.3 1.6 reshape.104
  39.9 1.7 multiply_convert_fusion.2
  41.6 20.2 %all-to-all-done.3 = bf16[128,4,2048]{0,2,1:T(8,128)(2,1)S(1)} async-done(((bf16[128,4,2048]{0,2,1:T(8,128)(2,1)}), bf16[128,4,2048]{0,2,1:T(8,128)(2,1)S(1)}, u32[]{:S(2)}, u32[]{:S(2)}) %all-to-all-start.3) | async-done | bytes 2097184 | tf_op jit(solution)/shard_map/all_to_all | solution.py:41
  61.8 10.7 %copy.96 = bf16[4,128,2048]{1,0,2:T(4,128)(2,1)} copy(bf16[4,128,2048]{1,2,0:T(8,128)(2,1)S(1)} %bitcast.81) | data formatting | bytes 4194304 | tf_op jit(solution)/shard_map/all_to_all | solution.py:41
  72.5 2.7 reshape.107
  75.2 2.1 fusion.10
  77.4 2.4 copy.142
  79.7 3.5 %all-to-all-start = ((bf16[128,4,1024]{2,0,1:T(8,128)(2,1)}), bf16[128,4,1024]{2,0,1:T(8,128)(2,1)S(1)}, u32[]{:S(2)}, u32[]{:S(2)}) async-start(bf16[128,4,1024]{2,0,1:T(8,128)(2,1)} %bitcast.85), calls=%async_computation | async-start | bytes 2097152 | tf_op jit(solution)/shard_map/all_to_all | solution.py:39
  83.3 4.1 %copy.106 = bf16[128,8192]{0,1:T(8,128)(2,1)} copy(bf16[128,8192]{1,0:T(8,128)(2,1)} %param.11) | data formatting | bytes 4194304 | tf_op args[3]
  87.4 0.1 iota_compare_fusion
  87.5 11.8 %all-gather.1 = f32[4,1,4]{2,1,0:T(1,128)S(1)} all-gather(f32[1,1,4]{2,1,0:T(1,128)S(1)} %bitcast.91), channel_id=1, replica_groups=mesh['groups'=2,'ctx'=4,'head'=4] {'ctx'}, dimensions={0}, use_global_device_ids=true | all-gather | bytes 80 | tf_op jit(solution)/shard_map/all_gather | solution.py:12
  99.3 4.7 %all-to-all-start.4 = ((bf16[128,4,2048]{0,2,1:T(8,128)(2,1)}), bf16[128,4,2048]{0,2,1:T(8,128)(2,1)}, u32[]{:S(2)}, u32[]{:S(2)}) async-start(bf16[128,4,2048]{0,2,1:T(8,128)(2,1)} %bitcast.80), calls=%async_computation.4 | async-start | bytes 4194304 | tf_op jit(solution)/shard_map/all_to_all | solution.py:42
  104.0 1.9 reshape.103
  105.8 6.6 %fusion.8 = f32[4,512,512]{1,2,0:T(8,128)} fusion(bf16[512,4,512]{0,2,1:T(8,128)(2,1)} %copy-done, f32[4,512]{1,0:T(4,128)S(1)} %bitcast.89, pred[512,512]{1,0:T(8,128)(4,1)S(1)} %iota_compare_fusion, bf16[512,4,256]{2,1,0:T(4,128)(2,1)} %reshape.104, bf16[512,4,256]{2,1,0:T(4,128)(2,1)S(1)} %reshape.103), kind=kOutput, calls=%fused_computation.19 | convolution fusion | flops 1616904192 | bytes 8658944 | tf_op jit(solution)/shard_map/hij,jhd->ihd/dot_general | solution.py:66
  112.4 115.5 %all-gather.4.cloned.1.call-done = f32[16,256,512]{2,1,0:T(8,128)} async-done(((f32[4,256,512]{2,1,0:T(8,128)}), f32[16,256,512]{2,1,0:T(8,128)}) %all-gather.4.cloned.1.call-update) | async-done | bytes 8388624 | tf_op jit(solution)/shard_map/all_gather | solution.py:12
  227.9 10.7 %while.14 = (s32[]{:T(128)}, f32[4,256,512]{2,1,0:T(8,128)S(1)}, s32[]{:T(128)}, f32[4,4]{1,0:T(4,128)S(1)}, f32[4,4,256,512]{3,2,1,0:T(8,128)}, /*index=5*/s32[]{:T(128)}, s32[]{:T(128)}) while((s32[]{:T(128)}, f32[4,256,512]{2,1,0:T(8,128)S(1)}, s32[]{:T(128)}, f32[4,4]{1,0:T(4,128)S(1)}, f32[4,4,256,512]{3,2,1,0:T(8,128)}, ...), condition=%wide.region_3.4_spmd.clone, body=%wide.region_2.3_spmd.clone.sunk | while | flops 2097156 | bytes 6291617 | solution.py:22
  227.9 2.6 fusion.30
  230.6 2.6 fusion.30
  233.3 2.6 fusion.30
  235.9 2.6 fusion.30
  238.6 0.1 convert_element_type.57
  238.7 0.3 fusion.9
  239.1 0.8 fusion.15
  239.9 0.8 fusion.17
  240.8 1.3 copy-done.2
  242.1 1.5 fusion.24
  243.6 0.5 multiply_reduce_fusion
  244.2 2.5 fusion.7
  246.7 5.2 %reshape.109 = f32[4,128,2048]{1,0,2:T(4,128)} reshape(f32[512,4,512]{0,2,1:T(8,128)} %fusion.7) | data formatting | bytes 8388608 | tf_op jit(solution)/shard_map/convert_element_type | solution.py:82
  251.9 3.9 %fusion.6 = bf16[4,128,2048]{1,2,0:T(8,128)(2,1)S(1)} fusion(bf16[128,4,2048]{0,2,1:T(8,128)(2,1)} %all-to-all-done.4, f32[4,128,2048]{1,0,2:T(4,128)} %reshape.109), kind=kLoop, calls=%fused_computation.14 | loop fusion | flops 7340032 | bytes 8388608 | tf_op jit(solution)/shard_map/convert_element_type | solution.py:82
  255.8 28.3 %all_to_all.90 = bf16[4,128,2048]{1,2,0:T(8,128)(2,1)S(1)} all-to-all(bf16[4,128,2048]{1,2,0:T(8,128)(2,1)S(1)} %fusion.6), channel_id=1, replica_groups=mesh['groups'=2,'ctx'=4,'head'=4] {'head'}, dimensions={0} | all-to-all | bytes 4194304 | tf_op jit(solution)/shard_map/all_to_all | solution.py:85
  284.1 2.9 copy.108
  (21 shorter events, 0.1 us)
Async XLA Ops:
  6.5 8.0 %all-to-all-start.2 = ((bf16[128,4,4]{0,2,1:T(4,128)(2,1)}), bf16[128,4,4]{0,2,1:T(4,128)(2,1)S(1)}, u32[]{:S(2)}, u32[]{:S(2)}) async-start(bf16[128,4,4]{0,2,1:T(4,128)(2,1)} %bitcast.92), calls=%async_computation.2 | async-start | bytes 8192 | tf_op jit(solution)/shard_map/all_to_all | solution.py:43
  14.5 18.0 %all-to-all-start.1 = ((bf16[128,4,1024]{2,0,1:T(8,128)(2,1)}), bf16[128,4,1024]{2,0,1:T(8,128)(2,1)S(1)}, u32[]{:S(2)}, u32[]{:S(2)}) async-start(bf16[128,4,1024]{2,0,1:T(8,128)(2,1)} %copy.92), calls=%async_computation.1 | async-start | bytes 2097152 | tf_op jit(solution)/shard_map/all_to_all | solution.py:40
  32.5 29.3 %all-to-all-start.3 = ((bf16[128,4,2048]{0,2,1:T(8,128)(2,1)}), bf16[128,4,2048]{0,2,1:T(8,128)(2,1)S(1)}, u32[]{:S(2)}, u32[]{:S(2)}) async-start(bf16[128,4,2048]{0,2,1:T(8,128)(2,1)} %bitcast.7), calls=%async_computation.3 | async-start | bytes 4194304 | tf_op jit(solution)/shard_map/all_to_all | solution.py:41
  36.1 191.8 %all-gather.4.cloned.1.call-start = ((), (), s32[]{:S(2)}) async-start(), calls=%async_computation.6 | async-start | bytes 10485760 | tf_op jit(solution)/shard_map/all_gather | solution.py:12
  75.2 4.5 %copy-start = (bf16[512,4,512]{0,2,1:T(8,128)(2,1)}, bf16[512,4,512]{0,2,1:T(8,128)(2,1)S(1)}, u32[]{:S(2)}) copy-start(bf16[512,4,512]{0,2,1:T(8,128)(2,1)S(1)} %reshape.107) | copy-start | bytes 6291460
  77.3 5.9 %copy-start.3 = (f32[2048]{0:T(1024)S(1)}, f32[2048]{0:T(1024)}, u32[]{:S(2)}) copy-start(f32[2048]{0:T(1024)} %param.13) | copy-start | bytes 24580
  79.7 19.6 %all-to-all-start = ((bf16[128,4,1024]{2,0,1:T(8,128)(2,1)}), bf16[128,4,1024]{2,0,1:T(8,128)(2,1)S(1)}, u32[]{:S(2)}, u32[]{:S(2)}) async-start(bf16[128,4,1024]{2,0,1:T(8,128)(2,1)} %bitcast.85), calls=%async_computation | async-start | bytes 2097152 | tf_op jit(solution)/shard_map/all_to_all | solution.py:39
  99.3 4.7 %copy-start.1 = (bf16[128,4,1024]{2,0,1:T(8,128)(2,1)}, bf16[128,4,1024]{2,0,1:T(8,128)(2,1)S(1)}, u32[]{:S(2)}) copy-start(bf16[128,4,1024]{2,0,1:T(8,128)(2,1)S(1)} %all-to-all-done) | copy-start | bytes 3145732
  99.3 152.6 %all-to-all-start.4 = ((bf16[128,4,2048]{0,2,1:T(8,128)(2,1)}), bf16[128,4,2048]{0,2,1:T(8,128)(2,1)}, u32[]{:S(2)}, u32[]{:S(2)}) async-start(bf16[128,4,2048]{0,2,1:T(8,128)(2,1)} %bitcast.80), calls=%async_computation.4 | async-start | bytes 4194304 | tf_op jit(solution)/shard_map/all_to_all | solution.py:42
  239.9 2.2 copy-start.2
Sparse Core Ops, SparseCore 0:
  77.5 150.3 all-gather.3
where the time goes:
time: 295 us; the launch traced here: 294 us
  waiting for transfers between devices  147 us (50%)
  local copies, waits for them, and re-layouts  40.4 us (14%)
  blocking collectives  40.1 us (14%)
  other arithmetic  21.4 us (7%)
  starting transfers between devices  19.5 us (7%)
  between operations  13.6 us (5%)
  matrix products  11.8 us (4%)
    all_gather x1, waiting for transfers between devices, prefix(): everything = jax.tree.map(lambda part: lax.all_gather(part, axis), x)  116 us
    all_to_all x1, blocking collectives, body(): lax.all_to_all(mixed, 'head', split_axis=0, concat_axis=1, tiled=True)  28.3 us
    all_to_all x1, waiting for transfers between devices, body(): lax.all_to_all(value_rows, 'head', split_axis=1, concat_axis=0, tiled=True)  20.2 us
    all_gather x1, blocking collectives, prefix(): everything = jax.tree.map(lambda part: lax.all_gather(part, axis), x)  11.8 us
    unnamed x12, local copies, waits for them, and re-layouts  11.1 us
    all_to_all x1, local copies, waits for them, and re-layouts, body(): lax.all_to_all(value_rows, 'head', split_axis=1, concat_axis=0, tiled=True)  10.7 us
    select_n x4, other arithmetic, turn(): return jax.tree.map(lambda a, b: jnp.where(reached, a, b), new, before)  10.5 us
    all_to_all x1, waiting for transfers between devices, body(): lax.all_to_all(key_rows, 'head', split_axis=1, concat_axis=0, tiled=True)  10.4 us
  transfers between devices with their start and end apart: 6, of which 4 were waited for; matrix products, arithmetic and copies ran while one was open for 17% of the time, Pallas kernels for 0%

commit v1 on v0

v1 whole, which is shorter than its diff:
```python
import functools

import jax
import jax.numpy as jnp
from jax import lax
from jax.experimental import pallas as pl
from jax.experimental.pallas import tpu as pltpu
from jax.sharding import PartitionSpec as P

KEY_DIM = 256
VALUE_DIM = 512
ROWS = 64
MESH = pl.DeviceIdType.MESH


def wide(row, copies):
    return jnp.concatenate([row] * copies, axis=1)


def kernel(
    peers, blocks, heads,
    q_ref, k_ref, v_ref, g_ref, dec_ref, gain_ref, out_ref,
    tots, gains, wcol, wrow, local,
    pair, lone, chip, arrived, before, after, onward, carry, given,
    tot_send, tot_recv, gain_send, gain_recv, pair_send, pair_recv, chip_send, chip_recv,
    after_send, after_recv, carry_send, carry_recv, given_send, given_recv,
):
    chips = peers // 2
    owned = heads // peers
    half = heads // 2
    tokens = q_ref.shape[0]
    scale = KEY_DIM ** (-0.5)
    me = lax.axis_index("head")
    block = lax.axis_index("ctx")
    x, c = lax.div(me, 2), lax.rem(me, 2)
    sibling = x * 2 + (1 - c)

    barrier = pltpu.get_barrier_semaphore()
    for step in range(1, peers):
        pl.semaphore_signal(
            barrier, inc=1, device_id={"head": lax.rem(me + step, peers)}, device_id_type=MESH
        )

    @pl.when(block > 0)
    def _():
        pl.semaphore_signal(barrier, inc=1, device_id={"ctx": block - 1}, device_id_type=MESH)

    @pl.when(block < blocks - 1)
    def _():
        pl.semaphore_signal(barrier, inc=1, device_id={"ctx": block + 1}, device_id_type=MESH)

    neighbours = jnp.minimum(block, 1) + jnp.minimum(blocks - 1 - block, 1)
    pl.semaphore_wait(barrier, peers - 1 + neighbours)

    def copy_to(src, dst, send, recv, where):
        return pltpu.make_async_remote_copy(
            src_ref=src, dst_ref=dst, send_sem=send, recv_sem=recv,
            device_id=where, device_id_type=MESH,
        )

    dec = dec_ref[...]
    first = lax.broadcasted_iota(jnp.int32, (tokens, tokens), 0)
    second = lax.broadcasted_iota(jnp.int32, (tokens, tokens), 1)
    causal = first >= second
    lower = jnp.where(causal, 1.0, 0.0).astype(jnp.bfloat16)
    upper = jnp.where(first <= second, 1.0, 0.0).astype(jnp.bfloat16)
    ones = jnp.ones((tokens, 128), jnp.bfloat16)
    down = (((0,), (0,)), ((), ()))
    tots[me] = lax.dot_general(dec, ones, down, preferred_element_type=jnp.float32)
    gains[me] = gain_ref[...]

    def tot_copy(step, source):
        return copy_to(
            tots.at[source], tots.at[source], tot_send.at[step], tot_recv.at[source],
            {"head": lax.rem(me + step, peers)},
        )

    def gain_copy(step, source):
        return copy_to(
            gains.at[source], gains.at[source], gain_send.at[step], gain_recv.at[source],
            {"head": lax.rem(me + step, peers)},
        )

    for step in range(1, peers):
        tot_copy(step, me).start()
    for step in range(1, peers):
        gain_copy(step, me).start()

    within = jnp.dot(lower, dec, preferred_element_type=jnp.float32)
    wrow[...] = lax.dot_general(dec, upper, down, preferred_element_type=jnp.float32)
    for h in range(heads):
        wcol[h] = jnp.broadcast_to(within[:, h : h + 1], (tokens, 128))

    def columns(ref, h, size):
        return ref[:, pl.ds(pl.multiple_of(h * size, size), size)]

    def total(device, h, copies):
        return wide(tots[device, pl.ds(h, 1), :], copies)

    def chunk_state(h):
        fade = jnp.exp(tots[me, pl.ds(h, 1), :] - wcol[h])
        keys = columns(k_ref, h, KEY_DIM).astype(jnp.float32) * wide(fade, KEY_DIM // 128)
        return lax.dot_general(
            keys.astype(jnp.bfloat16), columns(v_ref, h, VALUE_DIM), down,
            preferred_element_type=jnp.float32,
        ).astype(jnp.bfloat16)

    def by_rows(body):
        def turn(n, nothing):
            body(pl.ds(pl.multiple_of(n * ROWS, ROWS), ROWS))
            return nothing

        lax.fori_loop(0, KEY_DIM // ROWS, turn, 0)

    def pair_copy(j):
        return copy_to(
            lone.at[j], pair.at[c, j], pair_send.at[j], pair_recv.at[j], {"head": sibling}
        )

    def chip_copy(there, i):
        return copy_to(
            chip.at[there * owned + i], arrived.at[x, i],
            chip_send.at[there * owned + i], chip_recv.at[x, i], {"head": there * 2 + c},
        )

    def far_first(t):
        return lax.rem(x + 1 + lax.div(t, owned), chips), lax.rem(t, owned)

    def join_pair(t):
        there, i = far_first(t)
        j = there * owned + i
        h = (there * 2 + c) * owned + i
        copy_to(
            lone.at[j], pair.at[1 - c, j], pair_send.at[j], pair_recv.at[j], {"head": sibling}
        ).wait_recv()
        fade = jnp.exp(total(x * 2 + 1, h, VALUE_DIM // 128))

        def joined(rows):
            return (
                fade * pair[0, j, rows, :].astype(jnp.float32)
                + pair[1, j, rows, :].astype(jnp.float32)
            ).astype(jnp.bfloat16)

        @pl.when(there == x)
        def _():
            def put(rows):
                arrived[x, i, rows, :] = joined(rows)

            by_rows(put)

        @pl.when(there != x)
        def _():
            def put(rows):
                chip[j, rows, :] = joined(rows)

            by_rows(put)
            chip_copy(there, i).start()

    def states(t, nothing):
        there, i = far_first(t)
        j = there * owned + i
        lone[j] = chunk_state((there * 2 + (1 - c)) * owned + i)
        pair_copy(j).start()
        pair[c, j] = chunk_state((there * 2 + c) * owned + i)

        @pl.when(t == 0)
        def _():
            for step in range(1, peers):
                tot_copy(step, lax.rem(me + step, peers)).wait_recv()

        @pl.when(t > 0)
        def _():
            join_pair(t - 1)

        return nothing

    lax.fori_loop(0, half, states, 0)
    join_pair(half - 1)

    def inside(h):
        gaps = wcol[h] - wrow[pl.ds(h, 1), :]
        damping = jnp.where(causal, jnp.exp(jnp.where(causal, gaps, 0.0)), 0.0)
        scores = lax.dot_general(
            columns(q_ref, h, KEY_DIM), columns(k_ref, h, KEY_DIM), (((1,), (1,)), ((), ())),
            preferred_element_type=jnp.float32,
        )
        weights = (scores * scale * damping).astype(jnp.bfloat16)
        local[:, pl.ds(pl.multiple_of(h * VALUE_DIM, VALUE_DIM), VALUE_DIM)] = jnp.dot(
            weights, columns(v_ref, h, VALUE_DIM), preferred_element_type=jnp.float32
        )

    def after_copy(i):
        return copy_to(
            after.at[i], before.at[i], after_send.at[i], after_recv.at[i], {"ctx": block + 1}
        )

    def carry_copy(there, i):
        return copy_to(
            onward.at[there, i], carry.at[0, x * owned + i],
            carry_send.at[there, i], carry_recv.at[x * owned + i], {"head": there * 2 + c},
        )

    def own_heads(i, nothing):
        h = me * owned + i
        for step in range(1, chips):
            there = lax.rem(x + step, chips)
            copy_to(
                chip.at[there * owned + i], arrived.at[there, i],
                chip_send.at[there * owned + i], chip_recv.at[there, i], {"head": there * 2 + c},
            ).wait_recv()

        @pl.when(block > 0)
        def _():
            copy_to(
                after.at[i], before.at[i], after_send.at[i], after_recv.at[i], {"ctx": block - 1}
            ).wait_recv()

        @pl.when(block == 0)
        def _():
            before[i] = jnp.zeros((KEY_DIM, VALUE_DIM), jnp.bfloat16)

        fades = [
            jnp.exp(total(2 * n, h, VALUE_DIM // 128) + total(2 * n + 1, h, VALUE_DIM // 128))
            for n in range(chips)
        ]

        def put(rows):
            state = before[i, rows, :].astype(jnp.float32)
            for n in range(chips):
                onward[n, i, rows, :] = state.astype(jnp.bfloat16)
                state = fades[n] * state + arrived[n, i, rows, :].astype(jnp.float32)
            after[i, rows, :] = state.astype(jnp.bfloat16)

        by_rows(put)

        @pl.when(block < blocks - 1)
        def _():
            after_copy(i).start()

        for step in range(1, chips):
            carry_copy(lax.rem(x + step, chips), i).start()
        carry[0, x * owned + i] = onward[x, i]

        def local_head(n, nothing):
            inside(i * peers + n)
            return nothing

        lax.fori_loop(0, peers, local_head, 0)
        return nothing

    lax.fori_loop(0, owned, own_heads, 0)

    for step in range(1, peers):
        gain_copy(step, lax.rem(me + step, peers)).wait_recv()

    def finish(device, i, state):
        h = device * owned + i
        inter = jnp.dot(columns(q_ref, h, KEY_DIM), state, preferred_element_type=jnp.float32)
        rise = jnp.exp(wcol[h]) * scale
        retained = columns(local, h, VALUE_DIM) + inter * wide(rise, VALUE_DIM // 128)
        centered = retained - jnp.mean(retained, axis=-1, keepdims=True)
        spread = jnp.mean(centered * centered, axis=-1, keepdims=True)
        gain = gains[device, :, pl.ds(pl.multiple_of(i * VALUE_DIM, VALUE_DIM), VALUE_DIM)]
        normed = (centered * lax.rsqrt(spread + 1e-06) * gain).astype(jnp.bfloat16)
        gate = columns(g_ref, h, VALUE_DIM).astype(jnp.float32)
        out_ref[:, pl.ds(pl.multiple_of(h * VALUE_DIM, VALUE_DIM), VALUE_DIM)] = (
            normed.astype(jnp.float32) * (gate / (1.0 + jnp.exp(-gate)))
        ).astype(jnp.bfloat16)

    def near_first(t):
        return lax.rem(x + lax.rem(t, chips), chips), lax.div(t, chips)

    def given_copy(j):
        return copy_to(
            carry.at[1 - c, j], given.at[j], given_send.at[j], given_recv.at[j],
            {"head": sibling},
        )

    def take_given(t):
        there, i = near_first(t)
        j = there * owned + i
        given_copy(j).wait_recv()
        finish(there * 2 + (1 - c), i, given[j])

    def spread_carry(t, nothing):
        there, i = near_first(t)
        j = there * owned + i
        h = (there * 2 + c) * owned + i

        @pl.when(there != x)
        def _():
            copy_to(
                onward.at[there, i], carry.at[0, j], carry_send.at[there, i], carry_recv.at[j],
                {"head": there * 2 + c},
            ).wait_recv()

        fade = jnp.exp(total(x * 2, h, VALUE_DIM // 128))

        def put(rows):
            carry[1, j, rows, :] = (
                fade * carry[0, j, rows, :].astype(jnp.float32)
                + pair[0, j, rows, :].astype(jnp.float32)
            ).astype(jnp.bfloat16)

        by_rows(put)
        given_copy(j).start()
        finish(there * 2 + c, i, carry[c, j])

        @pl.when(t > 0)
        def _():
            take_given(t - 1)

        return nothing

    lax.fori_loop(0, half, spread_carry, 0)
    take_given(half - 1)

    for step in range(1, peers):
        tot_copy(step, me).wait_send()
        gain_copy(step, me).wait_send()

    def sent(j, nothing):
        pair_copy(j).wait_send()
        given_copy(j).wait_send()
        return nothing

    lax.fori_loop(0, half, sent, 0)

    def sent_far(i, nothing):
        for step in range(1, chips):
            there = lax.rem(x + step, chips)
            chip_copy(there, i).wait_send()
            carry_copy(there, i).wait_send()

        @pl.when(block < blocks - 1)
        def _():
            after_copy(i).wait_send()

        return nothing

    lax.fori_loop(0, owned, sent_far, 0)


def body(peers, blocks, query_rows, key_rows, value_rows, gate_rows, decay_log, norm_gain):
    tokens, heads = decay_log.shape
    chips, owned, half = peers // 2, heads // peers, heads // 2
    state = (KEY_DIM, VALUE_DIM)
    dma = pltpu.SemaphoreType.DMA
    width = norm_gain.shape[0]
    return pl.pallas_call(
        functools.partial(kernel, peers, blocks, heads),
        out_shape=jax.ShapeDtypeStruct(value_rows.shape, jnp.bfloat16),
        in_specs=[pl.BlockSpec(memory_space=pltpu.VMEM)] * 6,
        out_specs=pl.BlockSpec(memory_space=pltpu.VMEM),
        scratch_shapes=[
            pltpu.VMEM((peers, heads, 128), jnp.float32),
            pltpu.VMEM((peers, 1, width), jnp.float32),
            pltpu.VMEM((heads, tokens, 128), jnp.float32),
            pltpu.VMEM((heads, tokens), jnp.float32),
            pltpu.VMEM((tokens, heads * VALUE_DIM), jnp.float32),
            pltpu.VMEM((2, half) + state, jnp.bfloat16),
            pltpu.VMEM((half,) + state, jnp.bfloat16),
            pltpu.VMEM((half,) + state, jnp.bfloat16),
            pltpu.VMEM((chips, owned) + state, jnp.bfloat16),
            pltpu.VMEM((owned,) + state, jnp.bfloat16),
            pltpu.VMEM((owned,) + state, jnp.bfloat16),
            pltpu.VMEM((chips, owned) + state, jnp.bfloat16),
            pltpu.VMEM((2, half) + state, jnp.bfloat16),
            pltpu.VMEM((half,) + state, jnp.bfloat16),
            dma((peers,)), dma((peers,)), dma((peers,)), dma((peers,)),
            dma((half,)), dma((half,)), dma((half,)), dma((chips, owned)),
            dma((owned,)), dma((owned,)), dma((chips, owned)), dma((half,)),
            dma((half,)), dma((half,)),
        ],
        compiler_params=pltpu.CompilerParams(
            collective_id=0, has_side_effects=True, vmem_limit_bytes=52 * 1024 * 1024
        ),
    )(query_rows, key_rows, value_rows, gate_rows, decay_log, norm_gain.reshape(1, width))


def solution(mesh):
    rows = P(("groups", "ctx", "head"), None)
    return jax.shard_map(
        functools.partial(body, mesh.shape["head"], mesh.shape["ctx"]),
        mesh=mesh,
        in_specs=(rows, rows, rows, rows, rows, P("head")),
        out_specs=rows,
        check_vma=False,
    )
```

time: 295 us -> 67.8 us (0.23)
  the two profiles are of different devices: /device:TPU:0 before, /device:TPU:27 now
where the time goes in v1:
time: 67.8 us; the launch traced here: 67.5 us
  Pallas kernels  61.7 us (91%)
  local copies, waits for them, and re-layouts  5.82 us (9%)
    pallas_call x1, Pallas kernels, body(): pl.pallas_call(functools.partial(kernel, peers, blocks, heads), out_shape...  61.7 us
    unnamed x6, local copies, waits for them, and re-layouts  5.82 us

profile of v1, /device:TPU:27, one launch (start us, length us, event | category | flops | bytes accessed | tf_op | source)
XLA Modules:
  0.0 67.5 jit_solution(5659319529369241500)
XLA Ops:
  0.0 0.8 %copy.7.dec_ref = bf16[128,16]{1,0:T(8,128)(2,1)S(1)} copy(bf16[128,16]{0,1:T(8,128)(2,1)} %param.10) | data formatting | bytes 8192 | tf_op args[4]
  0.8 0.0 copy-start
  0.8 1.2 %copy-done = bf16[128,4096]{1,0:T(8,128)(2,1)S(1)} copy-done((bf16[128,4096]{1,0:T(8,128)(2,1)S(1)}, bf16[128,4096]{1,0:T(8,128)(2,1)}, u32[]{:S(2)}) %copy-start) | copy-done | bytes 1048600
  2.0 0.0 copy-start.1
  2.0 0.7 %copy-done.1 = f32[2048]{0:T(1024)S(1)} copy-done((f32[2048]{0:T(1024)S(1)}, f32[2048]{0:T(1024)}, u32[]{:S(2)}) %copy-start.1) | copy-done | bytes 8216
  2.7 61.7 %shard_map.64 = bf16[128,8192]{1,0:T(8,128)(2,1)} custom-call(bf16[128,4096]{1,0:T(8,128)(2,1)S(1)} %copy-done, bf16[128,4096]{1,0:T(8,128)(2,1)} %k_ref.1, bf16[128,8192]{1,0:T(8,128)(2,1)} %v_ref.1, bf16[128,8192]{1,0:T(8,128)(2,1)} %g_ref.1, bf16[128,16]{1,0:T(8,128)(2,1)S(1)} %copy.7.dec_ref, f32[1,2048]{1,0:T(1,128)S(1)} %bitcast.1), custom_call_target="tpu_custom_call" | custom-call | tf_op jit(solution)/shard_map/pallas_call | solution.py:350
  64.4 3.1 %copy.9 = bf16[128,8192]{1,0:T(8,128)(2,1)} copy(bf16[128,8192]{1,0:T(8,128)(2,1)} %shard_map.64) | data formatting | bytes 4194304
Async XLA Ops:
  0.8 1.2 %copy-start = (bf16[128,4096]{1,0:T(8,128)(2,1)S(1)}, bf16[128,4096]{1,0:T(8,128)(2,1)}, u32[]{:S(2)}) copy-start(bf16[128,4096]{1,0:T(8,128)(2,1)} %q_ref.1) | copy-start | bytes 3145732
  2.0 0.7 %copy-start.1 = (f32[2048]{0:T(1024)S(1)}, f32[2048]{0:T(1024)}, u32[]{:S(2)}) copy-start(f32[2048]{0:T(1024)} %param.11) | copy-start | bytes 24580

commit v2 on v1

--- a/solution.py
+++ b/solution.py
@@ -10,6 +10,7 @@
 KEY_DIM = 256
 VALUE_DIM = 512
 ROWS = 64
+PIECES = 2
 MESH = pl.DeviceIdType.MESH
 
 
@@ -19,8 +20,8 @@
 
 def kernel(
     peers, blocks, heads,
-    q_ref, k_ref, v_ref, g_ref, dec_ref, gain_ref, out_ref,
-    tots, gains, wcol, wrow, local,
+    q_hbm, k_hbm, v_hbm, g_hbm, dec_ref, gain_ref, out_ref,
+    q_ref, k_ref, v_ref, g_ref, load_sem, tots, gains, wcol, wrow, local,
     pair, lone, chip, arrived, before, after, onward, carry, given,
     tot_send, tot_recv, gain_send, gain_recv, pair_send, pair_recv, chip_send, chip_recv,
     after_send, after_recv, carry_send, carry_recv, given_send, given_recv,
@@ -34,6 +35,16 @@
     block = lax.axis_index("ctx")
     x, c = lax.div(me, 2), lax.rem(me, 2)
     sibling = x * 2 + (1 - c)
+    last = blocks - 1
+
+    loads = [
+        pltpu.make_async_copy(source, target, load_sem.at[n])
+        for n, (source, target) in enumerate(
+            ((k_hbm, k_ref), (v_hbm, v_ref), (q_hbm, q_ref), (g_hbm, g_ref))
+        )
+    ]
+    for load in loads:
+        load.start()
 
     barrier = pltpu.get_barrier_semaphore()
     for step in range(1, peers):
@@ -45,12 +56,9 @@
     def _():
         pl.semaphore_signal(barrier, inc=1, device_id={"ctx": block - 1}, device_id_type=MESH)
 
-    @pl.when(block < blocks - 1)
+    @pl.when(block < last)
     def _():
         pl.semaphore_signal(barrier, inc=1, device_id={"ctx": block + 1}, device_id_type=MESH)
-
-    neighbours = jnp.minimum(block, 1) + jnp.minimum(blocks - 1 - block, 1)
-    pl.semaphore_wait(barrier, peers - 1 + neighbours)
 
     def copy_to(src, dst, send, recv, where):
         return pltpu.make_async_remote_copy(
@@ -81,15 +89,18 @@
             {"head": lax.rem(me + step, peers)},
         )
 
+    within = jnp.dot(lower, dec, preferred_element_type=jnp.float32)
+    wrow[...] = lax.dot_general(dec, upper, down, preferred_element_type=jnp.float32)
+    for h in range(heads):
+        wcol[h] = jnp.broadcast_to(within[:, h : h + 1], (tokens, 128))
+
+    neighbours = jnp.minimum(block, 1) + jnp.minimum(blocks - 1 - block, 1)
+    pl.semaphore_wait(barrier, peers - 1 + neighbours)
+
     for step in range(1, peers):
         tot_copy(step, me).start()
     for step in range(1, peers):
         gain_copy(step, me).start()
-
-    within = jnp.dot(lower, dec, preferred_element_type=jnp.float32)
-    wrow[...] = lax.dot_general(dec, upper, down, preferred_element_type=jnp.float32)
-    for h in range(heads):
-        wcol[h] = jnp.broadcast_to(within[:, h : h + 1], (tokens, 128))
 
     def columns(ref, h, size):
         return ref[:, pl.ds(pl.multiple_of(h * size, size), size)]
@@ -112,57 +123,66 @@
 
         lax.fori_loop(0, KEY_DIM // ROWS, turn, 0)
 
+    def piece(p):
+        return pl.ds(p * (KEY_DIM // PIECES), KEY_DIM // PIECES)
+
+    def by_piece_rows(p, body):
+        size = KEY_DIM // PIECES
+
+        def turn(n, nothing):
+            body(pl.ds(pl.multiple_of(p * size + n * ROWS, ROWS), ROWS))
+            return nothing
+
+        lax.fori_loop(0, size // ROWS, turn, 0)
+
     def pair_copy(j):
         return copy_to(
             lone.at[j], pair.at[c, j], pair_send.at[j], pair_recv.at[j], {"head": sibling}
         )
 
-    def chip_copy(there, i):
-        return copy_to(
-            chip.at[there * owned + i], arrived.at[x, i],
-            chip_send.at[there * owned + i], chip_recv.at[x, i], {"head": there * 2 + c},
-        )
-
-    def far_first(t):
-        return lax.rem(x + 1 + lax.div(t, owned), chips), lax.rem(t, owned)
-
-    def join_pair(t):
-        there, i = far_first(t)
+    def chip_copy(there, i, p):
+        j = there * owned + i
+        return copy_to(
+            chip.at[j, piece(p)], arrived.at[x, i, piece(p)],
+            chip_send.at[j, p], chip_recv.at[x, i, p], {"head": there * 2 + c},
+        )
+
+    def join_pair(there, i, far):
         j = there * owned + i
         h = (there * 2 + c) * owned + i
         copy_to(
             lone.at[j], pair.at[1 - c, j], pair_send.at[j], pair_recv.at[j], {"head": sibling}
         ).wait_recv()
         fade = jnp.exp(total(x * 2 + 1, h, VALUE_DIM // 128))
-
-        def joined(rows):
-            return (
-                fade * pair[0, j, rows, :].astype(jnp.float32)
-                + pair[1, j, rows, :].astype(jnp.float32)
-            ).astype(jnp.bfloat16)
-
-        @pl.when(there == x)
-        def _():
+        for p in range(PIECES):
+
             def put(rows):
-                arrived[x, i, rows, :] = joined(rows)
-
-            by_rows(put)
-
-        @pl.when(there != x)
-        def _():
-            def put(rows):
-                chip[j, rows, :] = joined(rows)
-
-            by_rows(put)
-            chip_copy(there, i).start()
-
-    def states(t, nothing):
-        there, i = far_first(t)
+                joined = (
+                    fade * pair[0, j, rows, :].astype(jnp.float32)
+                    + pair[1, j, rows, :].astype(jnp.float32)
+                ).astype(jnp.bfloat16)
+                if far:
+                    chip[j, rows, :] = joined
+                else:
+                    arrived[x, i, rows, :] = joined
+
+            by_piece_rows(p, put)
+            if far:
+                chip_copy(there, i, p).start()
+
+    def states(there, i):
         j = there * owned + i
         lone[j] = chunk_state((there * 2 + (1 - c)) * owned + i)
         pair_copy(j).start()
         pair[c, j] = chunk_state((there * 2 + c) * owned + i)
 
+    def far_place(t):
+        return lax.rem(x + 1 + lax.rem(t, chips - 1), chips), lax.div(t, chips - 1)
+
+    def far_states(t, nothing):
+        there, i = far_place(t)
+        states(there, i)
+
         @pl.when(t == 0)
         def _():
             for step in range(1, peers):
@@ -170,12 +190,20 @@
 
         @pl.when(t > 0)
         def _():
-            join_pair(t - 1)
-
-        return nothing
-
-    lax.fori_loop(0, half, states, 0)
-    join_pair(half - 1)
+            before_there, before_i = far_place(t - 1)
+            join_pair(before_there, before_i, True)
+
+        return nothing
+
+    loads[0].wait()
+    loads[1].wait()
+    far = (chips - 1) * owned
+    lax.fori_loop(0, far, far_states, 0)
+    states(x, 0)
+    last_there, last_i = far_place(far - 1)
+    join_pair(last_there, last_i, True)
+    loads[2].wait()
+    loads[3].wait()
 
     def inside(h):
         gaps = wcol[h] - wrow[pl.ds(h, 1), :]
@@ -189,35 +217,39 @@
             weights, columns(v_ref, h, VALUE_DIM), preferred_element_type=jnp.float32
         )
 
-    def after_copy(i):
-        return copy_to(
-            after.at[i], before.at[i], after_send.at[i], after_recv.at[i], {"ctx": block + 1}
-        )
-
-    def carry_copy(there, i):
-        return copy_to(
-            onward.at[there, i], carry.at[0, x * owned + i],
-            carry_send.at[there, i], carry_recv.at[x * owned + i], {"head": there * 2 + c},
-        )
-
-    def own_heads(i, nothing):
+    def after_copy(i, p):
+        return copy_to(
+            after.at[i, piece(p)], before.at[i, piece(p)],
+            after_send.at[i, p], after_recv.at[i, p], {"ctx": block + 1},
+        )
+
+    def carry_copy(there, i, p):
+        j = x * owned + i
+        return copy_to(
+            onward.at[there, i, piece(p)], carry.at[0, j, piece(p)],
+            carry_send.at[there, i, p], carry_recv.at[j, p], {"head": there * 2 + c},
+        )
+
+    def chain(i, p):
         h = me * owned + i
         for step in range(1, chips):
             there = lax.rem(x + step, chips)
             copy_to(
-                chip.at[there * owned + i], arrived.at[there, i],
-                chip_send.at[there * owned + i], chip_recv.at[there, i], {"head": there * 2 + c},
+                chip.at[there * owned + i, piece(p)], arrived.at[there, i, piece(p)],
+                chip_send.at[there * owned + i, p], chip_recv.at[there, i, p],
+                {"head": there * 2 + c},
             ).wait_recv()
 
         @pl.when(block > 0)
         def _():
             copy_to(
-                after.at[i], before.at[i], after_send.at[i], after_recv.at[i], {"ctx": block - 1}
+                after.at[i, piece(p)], before.at[i, piece(p)],
+                after_send.at[i, p], after_recv.at[i, p], {"ctx": block - 1},
             ).wait_recv()
 
         @pl.when(block == 0)
         def _():
-            before[i] = jnp.zeros((KEY_DIM, VALUE_DIM), jnp.bfloat16)
+            before[i, piece(p)] = jnp.zeros((KEY_DIM // PIECES, VALUE_DIM), jnp.bfloat16)
 
         fades = [
             jnp.exp(total(2 * n, h, VALUE_DIM // 128) + total(2 * n + 1, h, VALUE_DIM // 128))
@@ -231,27 +263,61 @@
                 state = fades[n] * state + arrived[n, i, rows, :].astype(jnp.float32)
             after[i, rows, :] = state.astype(jnp.bfloat16)
 
-        by_rows(put)
-
-        @pl.when(block < blocks - 1)
-        def _():
-            after_copy(i).start()
-
+        by_piece_rows(p, put)
+
+        @pl.when(block < last)
+        def _():
+            after_copy(i, p).start()
+
+        @pl.when(block == last)
+        def _():
+            send_carry(i, p)
+
+    def send_carry(i, p):
         for step in range(1, chips):
-            carry_copy(lax.rem(x + step, chips), i).start()
+            carry_copy(lax.rem(x + step, chips), i, p).start()
+
+    def send_carries(i, nothing):
+        for p in range(PIECES):
+            send_carry(i, p)
+        return nothing
+
+    def locals_of(i):
+        def local_head(n, nothing):
+            inside(n * owned + i)
+            return nothing
+
+        lax.fori_loop(0, peers, local_head, 0)
+
+    delay = jnp.maximum(owned - 1 - block, 0)
+
+    def own_heads(i, nothing):
+        @pl.when(block > 0)
+        def _():
+            locals_of(i)
+
+        join_pair(x, i, False)
+        for p in range(PIECES):
+            chain(i, p)
         carry[0, x * owned + i] = onward[x, i]
 
-        def local_head(n, nothing):
-            inside(i * peers + n)
-            return nothing
-
-        lax.fori_loop(0, peers, local_head, 0)
-        return nothing
-
-    lax.fori_loop(0, owned, own_heads, 0)
-
-    for step in range(1, peers):
-        gain_copy(step, lax.rem(me + step, peers)).wait_recv()
+        @pl.when(jnp.logical_and(block < last, i >= delay))
+        def _():
+            send_carries(i - delay, 0)
+
+        @pl.when(i < owned - 1)
+        def _():
+            states(x, i + 1)
+
+        @pl.when(block == 0)
+        def _():
+            locals_of(i)
+
+        @pl.when(jnp.logical_and(block == last, i > 0))
+        def _():
+            spread_all(i - 1, 0)
+
+        return nothing
 
     def finish(device, i, state):
         h = device * owned + i
@@ -267,53 +333,61 @@
             normed.astype(jnp.float32) * (gate / (1.0 + jnp.exp(-gate)))
         ).astype(jnp.bfloat16)
 
-    def near_first(t):
-        return lax.rem(x + lax.rem(t, chips), chips), lax.div(t, chips)
-
     def given_copy(j):
         return copy_to(
             carry.at[1 - c, j], given.at[j], given_send.at[j], given_recv.at[j],
             {"head": sibling},
         )
 
-    def take_given(t):
-        there, i = near_first(t)
+    def take_given(there, i):
         j = there * owned + i
         given_copy(j).wait_recv()
         finish(there * 2 + (1 - c), i, given[j])
 
-    def spread_carry(t, nothing):
-        there, i = near_first(t)
+    def spread(there, i, far):
         j = there * owned + i
         h = (there * 2 + c) * owned + i
-
-        @pl.when(there != x)
-        def _():
-            copy_to(
-                onward.at[there, i], carry.at[0, j], carry_send.at[there, i], carry_recv.at[j],
-                {"head": there * 2 + c},
-            ).wait_recv()
-
         fade = jnp.exp(total(x * 2, h, VALUE_DIM // 128))
-
-        def put(rows):
-            carry[1, j, rows, :] = (
-                fade * carry[0, j, rows, :].astype(jnp.float32)
-                + pair[0, j, rows, :].astype(jnp.float32)
-            ).astype(jnp.bfloat16)
-
-        by_rows(put)
+        for p in range(PIECES):
+            if far:
+                copy_to(
+                    onward.at[there, i, piece(p)], carry.at[0, j, piece(p)],
+                    carry_send.at[there, i, p], carry_recv.at[j, p], {"head": there * 2 + c},
+                ).wait_recv()
+
+            def put(rows):
+                carry[1, j, rows, :] = (
+                    fade * carry[0, j, rows, :].astype(jnp.float32)
+                    + pair[0, j, rows, :].astype(jnp.float32)
+                ).astype(jnp.bfloat16)
+
+            by_piece_rows(p, put)
         given_copy(j).start()
         finish(there * 2 + c, i, carry[c, j])
 
-        @pl.when(t > 0)
-        def _():
-            take_given(t - 1)
-
-        return nothing
-
-    lax.fori_loop(0, half, spread_carry, 0)
-    take_given(half - 1)
+    def spread_all(i, nothing):
+        spread(x, i, False)
+        take_given(x, i)
+
+        def turn(step, nothing):
+            there = lax.rem(x + step, chips)
+            spread(there, i, True)
+            take_given(there, i)
+            return nothing
+
+        lax.fori_loop(1, chips, turn, 0)
+        return nothing
+
+    for step in range(1, peers):
+        gain_copy(step, lax.rem(me + step, peers)).wait_recv()
+
+    lax.fori_loop(0, owned, own_heads, 0)
+
+    @pl.when(block < last)
+    def _():
+        lax.fori_loop(jnp.maximum(owned - delay, 0), owned, send_carries, 0)
+
+    lax.fori_loop(jnp.where(block == last, owned - 1, 0), owned, spread_all, 0)
 
     for step in range(1, peers):
         tot_copy(step, me).wait_send()
@@ -329,12 +403,14 @@
     def sent_far(i, nothing):
         for step in range(1, chips):
             there = lax.rem(x + step, chips)
-            chip_copy(there, i).wait_send()
-            carry_copy(there, i).wait_send()
-
-        @pl.when(block < blocks - 1)
-        def _():
-            after_copy(i).wait_send()
+            for p in range(PIECES):
+                chip_copy(there, i, p).wait_send()
+                carry_copy(there, i, p).wait_send()
+
+        @pl.when(block < last)
+        def _():
+            for p in range(PIECES):
+                after_copy(i, p).wait_send()
 
         return nothing
 
@@ -350,9 +426,15 @@
     return pl.pallas_call(
         functools.partial(kernel, peers, blocks, heads),
         out_shape=jax.ShapeDtypeStruct(value_rows.shape, jnp.bfloat16),
-        in_specs=[pl.BlockSpec(memory_space=pltpu.VMEM)] * 6,
+        in_specs=[pl.BlockSpec(memory_space=pl.ANY)] * 4
+        + [pl.BlockSpec(memory_space=pltpu.VMEM)] * 2,
         out_specs=pl.BlockSpec(memory_space=pltpu.VMEM),
         scratch_shapes=[
+            pltpu.VMEM(query_rows.shape, jnp.bfloat16),
+            pltpu.VMEM(key_rows.shape, jnp.bfloat16),
+            pltpu.VMEM(value_rows.shape, jnp.bfloat16),
+            pltpu.VMEM(gate_rows.shape, jnp.bfloat16),
+            dma((4,)),
             pltpu.VMEM((peers, heads, 128), jnp.float32),
             pltpu.VMEM((peers, 1, width), jnp.float32),
             pltpu.VMEM((heads, tokens, 128), jnp.float32),
@@ -368,12 +450,14 @@
             pltpu.VMEM((2, half) + state, jnp.bfloat16),
             pltpu.VMEM((half,) + state, jnp.bfloat16),
             dma((peers,)), dma((peers,)), dma((peers,)), dma((peers,)),
-            dma((half,)), dma((half,)), dma((half,)), dma((chips, owned)),
-            dma((owned,)), dma((owned,)), dma((chips, owned)), dma((half,)),
+            dma((half,)), dma((half,)),
+            dma((half, PIECES)), dma((chips, owned, PIECES)),
+            dma((owned, PIECES)), dma((owned, PIECES)),
+            dma((chips, owned, PIECES)), dma((half, PIECES)),
             dma((half,)), dma((half,)),
         ],
         compiler_params=pltpu.CompilerParams(
-            collective_id=0, has_side_effects=True, vmem_limit_bytes=52 * 1024 * 1024
+            collective_id=0, has_side_effects=True, vmem_limit_bytes=60 * 1024 * 1024
         ),
     )(query_rows, key_rows, value_rows, gate_rows, decay_log, norm_gain.reshape(1, width))
 

time: 67.8 us -> 64.9 us (0.957)
  the two profiles are of different devices: /device:TPU:27 before, /device:TPU:0 now
where the time goes in v2:
time: 64.9 us; the launch traced here: 64.3 us
  Pallas kernels  59.8 us (92%)
  local copies, waits for them, and re-layouts  4.5 us (7%)
    pallas_call x1, Pallas kernels, body(): pl.pallas_call(functools.partial(kernel, peers, blocks, heads), out_shape...  59.8 us
    unnamed x2, local copies, waits for them, and re-layouts  4.5 us

profile of v2, /device:TPU:0, one launch (start us, length us, event | category | flops | bytes accessed | tf_op | source)
XLA Modules:
  0.0 64.3 jit_solution(14002243001139900626)
XLA Ops:
  0.0 1.4 %copy.7.dec_ref = bf16[128,16]{1,0:T(8,128)(2,1)} copy(bf16[128,16]{0,1:T(8,128)(2,1)} %param.10) | data formatting | bytes 8192 | tf_op args[4]
  1.4 59.8 %shard_map.64 = bf16[128,8192]{1,0:T(8,128)(2,1)} custom-call(bf16[128,4096]{1,0:T(8,128)(2,1)} %q_hbm.1, bf16[128,4096]{1,0:T(8,128)(2,1)} %k_hbm.1, bf16[128,8192]{1,0:T(8,128)(2,1)} %v_hbm.1, bf16[128,8192]{1,0:T(8,128)(2,1)} %g_hbm.1, bf16[128,16]{1,0:T(8,128)(2,1)} %copy.7.dec_ref, f32[1,2048]{1,0:T(1,128)} %bitcast.1), custom_call_target="tpu_custom_call" | custom-call | tf_op jit(solution)/shard_map/pallas_call | solution.py:426
  61.2 3.1 %copy.9 = bf16[128,8192]{1,0:T(8,128)(2,1)} copy(bf16[128,8192]{1,0:T(8,128)(2,1)} %shard_map.64) | data formatting | bytes 4194304

commit v3 on v2

--- a/solution.py
+++ b/solution.py
@@ -11,6 +11,7 @@
 VALUE_DIM = 512
 ROWS = 64
 PIECES = 2
+PARTS = 8
 MESH = pl.DeviceIdType.MESH
 
 
@@ -20,8 +21,8 @@
 
 def kernel(
     peers, blocks, heads,
-    q_hbm, k_hbm, v_hbm, g_hbm, dec_ref, gain_ref, out_ref,
-    q_ref, k_ref, v_ref, g_ref, load_sem, tots, gains, wcol, wrow, local,
+    q_hbm, k_hbm, v_hbm, g_hbm, dec_hbm, gain_hbm, out_hbm,
+    q_ref, k_ref, v_ref, g_ref, dec_ref, out_ref, load_sem, out_sem, tots, gains, wcol, wrow, local,
     pair, lone, chip, arrived, before, after, onward, carry, given,
     tot_send, tot_recv, gain_send, gain_recv, pair_send, pair_recv, chip_send, chip_recv,
     after_send, after_recv, carry_send, carry_recv, given_send, given_recv,
@@ -40,7 +41,10 @@
     loads = [
         pltpu.make_async_copy(source, target, load_sem.at[n])
         for n, (source, target) in enumerate(
-            ((k_hbm, k_ref), (v_hbm, v_ref), (q_hbm, q_ref), (g_hbm, g_ref))
+            (
+                (dec_hbm, dec_ref), (k_hbm, k_ref), (v_hbm, v_ref),
+                (gain_hbm, gains.at[me]), (q_hbm, q_ref), (g_hbm, g_ref),
+            )
         )
     ]
     for load in loads:
@@ -66,6 +70,7 @@
             device_id=where, device_id_type=MESH,
         )
 
+    loads[0].wait()
     dec = dec_ref[...]
     first = lax.broadcasted_iota(jnp.int32, (tokens, tokens), 0)
     second = lax.broadcasted_iota(jnp.int32, (tokens, tokens), 1)
@@ -74,8 +79,7 @@
     upper = jnp.where(first <= second, 1.0, 0.0).astype(jnp.bfloat16)
     ones = jnp.ones((tokens, 128), jnp.bfloat16)
     down = (((0,), (0,)), ((), ()))
-    tots[me] = lax.dot_general(dec, ones, down, preferred_element_type=jnp.float32)
-    gains[me] = gain_ref[...]
+    tots[me] = jnp.dot(dec, ones, preferred_element_type=jnp.float32)
 
     def tot_copy(step, source):
         return copy_to(
@@ -89,18 +93,12 @@
             {"head": lax.rem(me + step, peers)},
         )
 
-    within = jnp.dot(lower, dec, preferred_element_type=jnp.float32)
-    wrow[...] = lax.dot_general(dec, upper, down, preferred_element_type=jnp.float32)
+    within = lax.dot_general(
+        lower, dec, (((1,), (1,)), ((), ())), preferred_element_type=jnp.float32
+    )
+    wrow[...] = jnp.dot(dec, upper, preferred_element_type=jnp.float32)
     for h in range(heads):
         wcol[h] = jnp.broadcast_to(within[:, h : h + 1], (tokens, 128))
-
-    neighbours = jnp.minimum(block, 1) + jnp.minimum(blocks - 1 - block, 1)
-    pl.semaphore_wait(barrier, peers - 1 + neighbours)
-
-    for step in range(1, peers):
-        tot_copy(step, me).start()
-    for step in range(1, peers):
-        gain_copy(step, me).start()
 
     def columns(ref, h, size):
         return ref[:, pl.ds(pl.multiple_of(h * size, size), size)]
@@ -170,6 +168,11 @@
             if far:
                 chip_copy(there, i, p).start()
 
+    def make_states(there, i):
+        j = there * owned + i
+        lone[j] = chunk_state((there * 2 + (1 - c)) * owned + i)
+        pair[c, j] = chunk_state((there * 2 + c) * owned + i)
+
     def states(there, i):
         j = there * owned + i
         lone[j] = chunk_state((there * 2 + (1 - c)) * owned + i)
@@ -179,31 +182,50 @@
     def far_place(t):
         return lax.rem(x + 1 + lax.rem(t, chips - 1), chips), lax.div(t, chips - 1)
 
+    def tot_arrived(source):
+        copy_to(
+            tots.at[source], tots.at[source], tot_send.at[0], tot_recv.at[source],
+            {"head": sibling},
+        ).wait_recv()
+
+    loads[1].wait()
+    loads[2].wait()
+    head_there, head_i = far_place(0)
+    make_states(head_there, head_i)
+    neighbours = jnp.minimum(block, 1) + jnp.minimum(blocks - 1 - block, 1)
+    pl.semaphore_wait(barrier, peers - 1 + neighbours)
+    for step in range(1, peers):
+        tot_copy(step, me).start()
+    pair_copy(head_there * owned + head_i).start()
+    tot_arrived(sibling)
+    join_pair(head_there, head_i, True)
+
     def far_states(t, nothing):
         there, i = far_place(t)
         states(there, i)
 
-        @pl.when(t == 0)
-        def _():
-            for step in range(1, peers):
-                tot_copy(step, lax.rem(me + step, peers)).wait_recv()
-
-        @pl.when(t > 0)
+        @pl.when(t > 1)
         def _():
             before_there, before_i = far_place(t - 1)
             join_pair(before_there, before_i, True)
 
         return nothing
 
-    loads[0].wait()
-    loads[1].wait()
     far = (chips - 1) * owned
-    lax.fori_loop(0, far, far_states, 0)
+    lax.fori_loop(1, far, far_states, 0)
     states(x, 0)
-    last_there, last_i = far_place(far - 1)
-    join_pair(last_there, last_i, True)
-    loads[2].wait()
-    loads[3].wait()
+    if far > 1:
+        last_there, last_i = far_place(far - 1)
+        join_pair(last_there, last_i, True)
+    for load in loads[3:]:
+        load.wait()
+    for step in range(1, peers):
+        gain_copy(step, me).start()
+    for source in range(peers):
+
+        @pl.when(x != source // 2)
+        def _():
+            tot_arrived(source)
 
     def inside(h):
         gaps = wcol[h] - wrow[pl.ds(h, 1), :]
@@ -269,18 +291,8 @@
         def _():
             after_copy(i, p).start()
 
-        @pl.when(block == last)
-        def _():
-            send_carry(i, p)
-
-    def send_carry(i, p):
         for step in range(1, chips):
             carry_copy(lax.rem(x + step, chips), i, p).start()
-
-    def send_carries(i, nothing):
-        for p in range(PIECES):
-            send_carry(i, p)
-        return nothing
 
     def locals_of(i):
         def local_head(n, nothing):
@@ -289,8 +301,6 @@
 
         lax.fori_loop(0, peers, local_head, 0)
 
-    delay = jnp.maximum(owned - 1 - block, 0)
-
     def own_heads(i, nothing):
         @pl.when(block > 0)
         def _():
@@ -301,10 +311,6 @@
             chain(i, p)
         carry[0, x * owned + i] = onward[x, i]
 
-        @pl.when(jnp.logical_and(block < last, i >= delay))
-        def _():
-            send_carries(i - delay, 0)
-
         @pl.when(i < owned - 1)
         def _():
             states(x, i + 1)
@@ -318,6 +324,12 @@
             spread_all(i - 1, 0)
 
         return nothing
+
+    def out_copy(h):
+        place = pl.ds(pl.multiple_of(h * VALUE_DIM, VALUE_DIM), VALUE_DIM)
+        return pltpu.make_async_copy(
+            out_ref.at[:, place], out_hbm.at[:, place], out_sem.at[h]
+        )
 
     def finish(device, i, state):
         h = device * owned + i
@@ -332,16 +344,18 @@
         out_ref[:, pl.ds(pl.multiple_of(h * VALUE_DIM, VALUE_DIM), VALUE_DIM)] = (
             normed.astype(jnp.float32) * (gate / (1.0 + jnp.exp(-gate)))
         ).astype(jnp.bfloat16)
-
-    def given_copy(j):
-        return copy_to(
-            carry.at[1 - c, j], given.at[j], given_send.at[j], given_recv.at[j],
-            {"head": sibling},
+        out_copy(h).start()
+
+    def given_copy(j, p):
+        return copy_to(
+            carry.at[1 - c, j, piece(p)], given.at[j, piece(p)],
+            given_send.at[j, p], given_recv.at[j, p], {"head": sibling},
         )
 
     def take_given(there, i):
         j = there * owned + i
-        given_copy(j).wait_recv()
+        for p in range(PIECES):
+            given_copy(j, p).wait_recv()
         finish(there * 2 + (1 - c), i, given[j])
 
     def spread(there, i, far):
@@ -362,7 +376,7 @@
                 ).astype(jnp.bfloat16)
 
             by_piece_rows(p, put)
-        given_copy(j).start()
+            given_copy(j, p).start()
         finish(there * 2 + c, i, carry[c, j])
 
     def spread_all(i, nothing):
@@ -383,11 +397,11 @@
 
     lax.fori_loop(0, owned, own_heads, 0)
 
-    @pl.when(block < last)
-    def _():
-        lax.fori_loop(jnp.maximum(owned - delay, 0), owned, send_carries, 0)
-
     lax.fori_loop(jnp.where(block == last, owned - 1, 0), owned, spread_all, 0)
+
+    def written(h, nothing):
+        out_copy(h).wait()
+        return nothing
 
     for step in range(1, peers):
         tot_copy(step, me).wait_send()
@@ -395,7 +409,8 @@
 
     def sent(j, nothing):
         pair_copy(j).wait_send()
-        given_copy(j).wait_send()
+        for p in range(PIECES):
+            given_copy(j, p).wait_send()
         return nothing
 
     lax.fori_loop(0, half, sent, 0)
@@ -415,6 +430,21 @@
         return nothing
 
     lax.fori_loop(0, owned, sent_far, 0)
+    lax.fori_loop(0, heads, written, 0)
+
+
+def rewrite(source, target, sem):
+    rows = source.shape[0] // PARTS
+    copies = [
+        pltpu.make_async_copy(
+            source.at[pl.ds(n * rows, rows)], target.at[pl.ds(n * rows, rows)], sem.at[n]
+        )
+        for n in range(PARTS)
+    ]
+    for copy in copies:
+        copy.start()
+    for copy in copies:
+        copy.wait()
 
 
 def body(peers, blocks, query_rows, key_rows, value_rows, gate_rows, decay_log, norm_gain):
@@ -423,18 +453,19 @@
     state = (KEY_DIM, VALUE_DIM)
     dma = pltpu.SemaphoreType.DMA
     width = norm_gain.shape[0]
-    return pl.pallas_call(
+    retained = pl.pallas_call(
         functools.partial(kernel, peers, blocks, heads),
         out_shape=jax.ShapeDtypeStruct(value_rows.shape, jnp.bfloat16),
-        in_specs=[pl.BlockSpec(memory_space=pl.ANY)] * 4
-        + [pl.BlockSpec(memory_space=pltpu.VMEM)] * 2,
-        out_specs=pl.BlockSpec(memory_space=pltpu.VMEM),
+        in_specs=[pl.BlockSpec(memory_space=pl.ANY)] * 6,
+        out_specs=pl.BlockSpec(memory_space=pl.ANY),
         scratch_shapes=[
             pltpu.VMEM(query_rows.shape, jnp.bfloat16),
             pltpu.VMEM(key_rows.shape, jnp.bfloat16),
             pltpu.VMEM(value_rows.shape, jnp.bfloat16),
             pltpu.VMEM(gate_rows.shape, jnp.bfloat16),
-            dma((4,)),
+            pltpu.VMEM((heads, tokens), jnp.bfloat16),
+            pltpu.VMEM(value_rows.shape, jnp.bfloat16),
+            dma((6,)), dma((heads,)),
             pltpu.VMEM((peers, heads, 128), jnp.float32),
             pltpu.VMEM((peers, 1, width), jnp.float32),
             pltpu.VMEM((heads, tokens, 128), jnp.float32),
@@ -454,12 +485,19 @@
             dma((half, PIECES)), dma((chips, owned, PIECES)),
             dma((owned, PIECES)), dma((owned, PIECES)),
             dma((chips, owned, PIECES)), dma((half, PIECES)),
-            dma((half,)), dma((half,)),
+            dma((half, PIECES)), dma((half, PIECES)),
         ],
         compiler_params=pltpu.CompilerParams(
             collective_id=0, has_side_effects=True, vmem_limit_bytes=60 * 1024 * 1024
         ),
-    )(query_rows, key_rows, value_rows, gate_rows, decay_log, norm_gain.reshape(1, width))
+    )(query_rows, key_rows, value_rows, gate_rows, decay_log.T, norm_gain.reshape(1, width))
+    return pl.pallas_call(
+        rewrite,
+        out_shape=jax.ShapeDtypeStruct(retained.shape, retained.dtype),
+        in_specs=[pl.BlockSpec(memory_space=pl.ANY)],
+        out_specs=pl.BlockSpec(memory_space=pl.ANY),
+        scratch_shapes=[dma((PARTS,))],
+    )(retained)
 
 
 def solution(mesh):

time: 64.9 us -> 138 us (2.13)
  the two profiles are of different devices: /device:TPU:0 before, /device:TPU:16 now
where the time goes in v3:
time: 138 us
  Pallas kernels  138 us (100%)
    pallas_call x1, Pallas kernels, body(): pl.pallas_call(functools.partial(kernel, peers, blocks, heads), out_shape...  73.1 us
    pallas_call x1, Pallas kernels, body(): pl.pallas_call(rewrite, out_shape=jax.ShapeDtypeStruct(retained.shape, re...  64.7 us

profile of v3, /device:TPU:16, one launch (start us, length us, event | category | flops | bytes accessed | tf_op | source)
XLA Modules:
  0.0 137.8 jit_solution(12663451624905575106)
XLA Ops:
  0.0 73.1 %shard_map.64.source = bf16[128,8192]{1,0:T(8,128)(2,1)} custom-call(bf16[128,4096]{1,0:T(8,128)(2,1)} %q_hbm.1, bf16[128,4096]{1,0:T(8,128)(2,1)} %k_hbm.1, bf16[128,8192]{1,0:T(8,128)(2,1)} %v_hbm.1, bf16[128,8192]{1,0:T(8,128)(2,1)} %g_hbm.1, bf16[16,128]{1,0:T(8,128)(2,1)} %bitcast.3, f32[1,2048]{1,0:T(1,128)} %bitcast.2), custom_call_target="tpu_custom_call" | custom-call | tf_op jit(solution)/shard_map/pallas_call | solution.py:456
  73.1 64.7 %shard_map.65 = bf16[128,8192]{1,0:T(8,128)(2,1)} custom-call(bf16[128,8192]{1,0:T(8,128)(2,1)} %shard_map.64.source), custom_call_target="tpu_custom_call" | custom-call | tf_op jit(solution)/shard_map/pallas_call | solution.py:494

commit v4 on v3

--- a/solution.py
+++ b/solution.py
@@ -197,6 +197,9 @@
     for step in range(1, peers):
         tot_copy(step, me).start()
     pair_copy(head_there * owned + head_i).start()
+    loads[3].wait()
+    for step in range(1, peers):
+        gain_copy(step, me).start()
     tot_arrived(sibling)
     join_pair(head_there, head_i, True)
 
@@ -217,10 +220,8 @@
     if far > 1:
         last_there, last_i = far_place(far - 1)
         join_pair(last_there, last_i, True)
-    for load in loads[3:]:
+    for load in loads[4:]:
         load.wait()
-    for step in range(1, peers):
-        gain_copy(step, me).start()
     for source in range(peers):
 
         @pl.when(x != source // 2)
@@ -433,18 +434,24 @@
     lax.fori_loop(0, heads, written, 0)
 
 
-def rewrite(source, target, sem):
+def rewrite(source, target, stage, sem, out_sem):
     rows = source.shape[0] // PARTS
-    copies = [
-        pltpu.make_async_copy(
-            source.at[pl.ds(n * rows, rows)], target.at[pl.ds(n * rows, rows)], sem.at[n]
-        )
-        for n in range(PARTS)
+    parts = [pl.ds(n * rows, rows) for n in range(PARTS)]
+    reads = [
+        pltpu.make_async_copy(source.at[part], stage.at[part], sem.at[n])
+        for n, part in enumerate(parts)
     ]
-    for copy in copies:
-        copy.start()
-    for copy in copies:
-        copy.wait()
+    writes = [
+        pltpu.make_async_copy(stage.at[part], target.at[part], out_sem.at[n])
+        for n, part in enumerate(parts)
+    ]
+    for read in reads:
+        read.start()
+    for read, write in zip(reads, writes):
+        read.wait()
+        write.start()
+    for write in writes:
+        write.wait()
 
 
 def body(peers, blocks, query_rows, key_rows, value_rows, gate_rows, decay_log, norm_gain):
@@ -496,7 +503,9 @@
         out_shape=jax.ShapeDtypeStruct(retained.shape, retained.dtype),
         in_specs=[pl.BlockSpec(memory_space=pl.ANY)],
         out_specs=pl.BlockSpec(memory_space=pl.ANY),
-        scratch_shapes=[dma((PARTS,))],
+        scratch_shapes=[
+            pltpu.VMEM(retained.shape, retained.dtype), dma((PARTS,)), dma((PARTS,))
+        ],
     )(retained)
 
 

time: 138 us -> 58.7 us (0.43)
  the two profiles are of different devices: /device:TPU:16 before, /device:TPU:0 now
where the time goes in v4:
time: 58.7 us; the launch traced here: 58.5 us
  Pallas kernels  58.5 us (100%)
    pallas_call x1, Pallas kernels, body(): pl.pallas_call(functools.partial(kernel, peers, blocks, heads), out_shape...  56.1 us
    pallas_call x1, Pallas kernels, body(): pl.pallas_call(rewrite, out_shape=jax.ShapeDtypeStruct(retained.shape, re...  2.39 us

profile of v4, /device:TPU:0, one launch (start us, length us, event | category | flops | bytes accessed | tf_op | source)
XLA Modules:
  0.0 58.5 jit_solution(17630087160579313062)
XLA Ops:
  0.0 56.1 %shard_map.64.source = bf16[128,8192]{1,0:T(8,128)(2,1)} custom-call(bf16[128,4096]{1,0:T(8,128)(2,1)} %q_hbm.1, bf16[128,4096]{1,0:T(8,128)(2,1)} %k_hbm.1, bf16[128,8192]{1,0:T(8,128)(2,1)} %v_hbm.1, bf16[128,8192]{1,0:T(8,128)(2,1)} %g_hbm.1, bf16[16,128]{1,0:T(8,128)(2,1)} %bitcast.3, f32[1,2048]{1,0:T(1,128)} %bitcast.2), custom_call_target="tpu_custom_call" | custom-call | tf_op jit(solution)/shard_map/pallas_call | solution.py:463
  56.1 2.4 %shard_map.65 = bf16[128,8192]{1,0:T(8,128)(2,1)} custom-call(bf16[128,8192]{1,0:T(8,128)(2,1)} %shard_map.64.source), custom_call_target="tpu_custom_call" | custom-call | tf_op jit(solution)/shard_map/pallas_call | solution.py:501
